TPU v7x, 512 devices: a whole 4x8x8 slice. The times are simulated.
512 devices in a mesh: dp: 64 (over y_lo, x, z), space: 8 (over y_hi, core).
Axes of the slice: x: 4, y: 8 (y_hi: 4, y_lo: 2; y = y_hi * 2 + y_lo), z: 8, core: 2. Of those that a mesh axis runs over, the one named last changes fastest.
Arguments:
- field_in: bfloat16 [1, 512, 512, 128], P(None, 'space', 'dp'), may hold values from -6 to 6
- pre_act: bfloat16 [1, 512, 512, 128], P(None, 'space', 'dp'), may hold values from -8 to 8
- cotangent: bfloat16 [1, 512, 512, 128], P(None, 'space', 'dp'), may hold values from -6 to 6
- spec_weight: bfloat16 [64, 64, 2, 128, 128], P('dp', 'space'), may hold values from -0.25 to 0.25
- local_weight: bfloat16 [128, 128], replicated, may hold values from -0.5 to 0.5
Outputs:
- grad_input: bfloat16 [1, 512, 512, 128], P(None, 'space', 'dp')
- grad_spectral: bfloat16 [64, 64, 2, 128, 128], P('dp', 'space')
- grad_local: float32 [128, 128], replicated
- grad_bias: float32 [128], replicated
All inputs are finite; a program needn't handle non-finite values.
Results may differ from a plain program's by a relative error of at most 0.0075.
The roundings to bfloat16 on the way count: a program that leaves them out, or rounds other values in their place, can miss the bound.
Values may be sent and summed in bfloat16 or wider, within the bound.
A program may use at most 64 MiB of HBM per device.

v0:
```python
import math

import jax
import jax.numpy as jnp
from jax import lax
from jax.sharding import PartitionSpec as P

root_two_pi = 0.7978845608028654
cubic_coef = 0.044715


def gelu_slope(values):
    tangent = jnp.tanh(root_two_pi * (values + cubic_coef * values * values * values))
    return 0.5 * (1.0 + tangent) + 0.5 * values * (1.0 - tangent * tangent) * root_two_pi * (
        1.0 + 3.0 * cubic_coef * values * values
    )


def y_basis(grid_cols, ky_count):
    positions = jnp.arange(grid_cols, dtype=jnp.int32)
    frequency = jnp.arange(ky_count, dtype=jnp.int32)
    phases = positions[:, None] * frequency[None, :] % grid_cols
    angles = phases.astype(jnp.float32) * (2.0 * math.pi / grid_cols)
    basis_table = jnp.stack([jnp.cos(angles), -jnp.sin(angles)], axis=2).reshape(
        grid_cols, 2 * ky_count
    )
    return basis_table.astype(jnp.bfloat16)


def x_rows_table(positions, grid_rows, kx_count):
    mode_index = jnp.arange(kx_count, dtype=jnp.int32)
    frequency = jnp.where(mode_index < kx_count // 2, mode_index, mode_index - kx_count)
    phases = frequency[:, None] * positions[None, :] % grid_rows
    angles = phases.astype(jnp.float32) * (2.0 * math.pi / grid_rows)
    cosine = jnp.cos(angles)
    sine = jnp.sin(angles)
    upper_rows = jnp.stack([cosine, sine], axis=1)
    lower_rows = jnp.stack([-sine, cosine], axis=1)
    return jnp.stack([upper_rows, lower_rows], axis=0).astype(jnp.bfloat16)


def on_device(field_in, pre_act, cotangent, spec_weight, local_weight):
    batch_size, slab_rows, col_block, channels = field_in.shape
    space_count = lax.axis_size("space")
    data_count = lax.axis_size("dp")
    grid_rows = slab_rows * space_count
    grid_cols = col_block * data_count
    row_count = slab_rows // data_count
    held_count = space_count * row_count
    kx_local = spec_weight.shape[0]
    kx_count = kx_local * data_count
    ky_local = spec_weight.shape[1]
    ky_count = ky_local * space_count
    data_index = lax.axis_index("dp")
    space_index = lax.axis_index("space")
    y_table = y_basis(grid_cols, ky_count)
    held_rows = (
        jnp.arange(space_count, dtype=jnp.int32)[:, None] * slab_rows
        + data_index * row_count
        + jnp.arange(row_count, dtype=jnp.int32)[None, :]
    ).reshape(held_count)
    x_held = x_rows_table(held_rows, grid_rows, kx_count)
    delta_field = (cotangent.astype(jnp.float32) * gelu_slope(pre_act.astype(jnp.float32))).astype(
        jnp.bfloat16
    )
    local_term = jnp.einsum(
        "bxyc,bxyo->co", field_in, delta_field, preferred_element_type=jnp.float32
    )
    bias_term = jnp.sum(delta_field, axis=(0, 1, 2), dtype=jnp.float32)
    local_sum, bias_sum = lax.psum((local_term, bias_term), ("dp", "space"))
    stacked = jnp.stack([field_in, delta_field])
    lines = lax.all_to_all(stacked, "dp", split_axis=2, concat_axis=3, tiled=True)
    pairs = lax.all_to_all(
        jnp.einsum("fbxyc,yr->fbxrc", lines, y_table, preferred_element_type=jnp.float32).astype(
            jnp.bfloat16
        ),
        "space",
        split_axis=3,
        concat_axis=2,
        tiled=True,
    )
    field_count = pairs.shape[0]
    split_pairs = pairs.reshape(field_count, batch_size, held_count, ky_local, 2, channels)
    table = x_held
    owned = lax.psum_scatter(
        jnp.einsum("qjpx,fbxkpc->jfbkqc", table, split_pairs, preferred_element_type=jnp.float32),
        "dp",
        scatter_dimension=0,
        tiled=True,
    ).astype(jnp.bfloat16)
    input_owned = owned[:, 0]
    delta_owned = owned[:, 1]
    ky_index = space_index * ky_local + jnp.arange(ky_local, dtype=jnp.int32)
    ky_scale = jnp.where(ky_index == 0, 1.0, 2.0).astype(jnp.float32) / (grid_rows * grid_cols)
    products = jnp.einsum(
        "jbkqc,jbkpo->jkqpco", input_owned, delta_owned, preferred_element_type=jnp.float32
    )
    grad_real = products[:, :, 0, 0] + products[:, :, 1, 1]
    grad_imag = products[:, :, 0, 1] - products[:, :, 1, 0]
    grad_spectral = (
        jnp.stack([grad_real, grad_imag], axis=2)
        * (ky_scale / batch_size)[None, :, None, None, None]
    ).astype(jnp.bfloat16)
    adjoint = jnp.einsum(
        "jbkpo,jkqco->bjkpqc", delta_owned, spec_weight, preferred_element_type=jnp.float32
    )
    back_real = adjoint[:, :, :, 0, 0] + adjoint[:, :, :, 1, 1]
    back_imag = adjoint[:, :, :, 1, 0] - adjoint[:, :, :, 0, 1]
    mode_back = (
        jnp.stack([back_real, back_imag], axis=3) * ky_scale[None, None, :, None, None]
    ).astype(jnp.bfloat16)
    table = x_held
    along_x = jnp.einsum(
        "qjpx,bjkqc->bxkpc",
        table,
        lax.all_gather(mode_back, "dp", axis=1, tiled=True),
        preferred_element_type=jnp.float32,
    ).astype(jnp.bfloat16)
    along_x = along_x.reshape(batch_size, held_count, 2 * ky_local, channels)
    lines_back = lax.all_to_all(along_x, "space", split_axis=1, concat_axis=2, tiled=True)
    local_part = jnp.einsum(
        "bxyo,co->bxyc", delta_field, local_weight, preferred_element_type=jnp.float32
    )
    slab_lines = lax.all_gather(lines_back, "dp", axis=1, tiled=True)
    y_block = lax.dynamic_slice_in_dim(y_table, data_index * col_block, col_block, 0)
    spectral_part = jnp.einsum(
        "bxrc,yr->bxyc", slab_lines, y_block, preferred_element_type=jnp.float32
    ).astype(jnp.bfloat16)
    grad_input = (spectral_part.astype(jnp.float32) + local_part).astype(jnp.bfloat16)
    return (grad_input, grad_spectral, local_sum / batch_size, bias_sum / batch_size)


def solution(mesh):
    placed = (
        P(None, "space", "dp", None),
        P(None, "space", "dp", None),
        P(None, "space", "dp", None),
        P("dp", "space", None, None, None),
        P(),
    )
    return jax.shard_map(
        on_device,
        mesh=mesh,
        in_specs=placed,
        out_specs=(P(None, "space", "dp", None), P("dp", "space", None, None, None), P(), P()),
        check_vma=False,
    )
```

profile of v0, /device:TPU:16, one launch (start us, length us, event | category | flops | bytes accessed | tf_op | source)
XLA Modules:
  0.0 838.3 jit_solution(12355432250104961929)
XLA Ops:
  8.0 1.2 convert_reduce_fusion
  9.3 1.6 pad_maximum_fusion
  10.9 14.8 %all-to-all-start = ((bf16[2,1,64,8,128]{4,3,1,0,2:T(8,128)(2,1)}), bf16[2,1,64,8,128]{4,3,1,0,2:T(8,128)(2,1)S(1)}, u32[]{:S(2)}, u32[]{:S(2)}) async-start(bf16[2,1,64,8,128]{4,3,1,0,2:T(8,128)(2,1)} %pad_maximum_fusion), calls=%async_computation | async-start | bytes 524288 | tf_op jit(solution)/shard_map/all_to_all | solution.py:72
  25.7 0.5 sine_negate_fusion
  26.3 0.1 copy.82
  26.5 12.6 %all-to-all-done = bf16[2,1,64,8,128]{4,3,1,0,2:T(8,128)(2,1)S(1)} async-done(((bf16[2,1,64,8,128]{4,3,1,0,2:T(8,128)(2,1)}), bf16[2,1,64,8,128]{4,3,1,0,2:T(8,128)(2,1)S(1)}, u32[]{:S(2)}, u32[]{:S(2)}) %all-to-all-start) | async-done | bytes 262176 | tf_op jit(solution)/shard_map/all_to_all | solution.py:72
  39.2 0.2 fusion.16
  39.3 0.7 copy.85
  40.0 6.5 all-to-all-start.1
  46.6 0.1 fusion.59
  46.7 5.5 all-to-all-done.1
  52.3 0.3 convolution_bitcast_fusion
  52.6 1.6 copy.88
  54.2 311.5 %reduce-scatter.2.cloned.1.call-done = f32[1,2,1,8,2,128]{5,3,4,2,1,0:T(8,128)} async-done(((f32[64,2,1,8,2,128]{5,3,4,2,1,0:T(8,128)}), f32[1,2,1,8,2,128]{5,3,4,2,1,0:T(8,128)}) %reduce-scatter.2.cloned.1.call-update) | async-done | bytes 16400 | tf_op jit(solution)/shard_map/reduce_scatter | solution.py:85
  365.7 0.7 convert_element_type.130
  366.4 0.2 convolution_bitcast_fusion.4
  366.8 152.5 %all_gather.6 = bf16[1,64,8,2,128]{4,2,3,0,1:T(8,128)(2,1)S(1)} all-gather(bf16[1,1,8,2,128]{4,2,3,0,1:T(8,128)(2,1)S(1)} %fusion.55), channel_id=1, replica_groups=mesh['dp'=64,'space'=8] {'dp'}, dimensions={1}, use_global_device_ids=true | all-gather | bytes 266240 | tf_op jit(solution)/shard_map/all_gather | solution.py:116
  519.3 0.2 fusion.17
  519.5 0.6 copy.95
  520.1 6.3 all-to-all-start.2
  526.4 0.9 convolution_bitcast_fusion.2
  527.3 4.5 all-to-all-done.2
  531.9 0.6 copy-done.1
  532.6 96.2 %psum.15 = f32[128]{0:T(128)} all-reduce(f32[128]{0:T(128)S(1)} %get-tuple-element.28), channel_id=1, replica_groups=mesh['dp'=64,'space'=8] {'dp','space'}, use_global_device_ids=true, to_apply=%region_3.4 | all-reduce | flops 128 | bytes 1024 | tf_op jit(solution)/shard_map/psum | solution.py:70
  628.8 162.3 %all-reduce.2.cloned.1.call-done = f32[128,128]{0,1:T(8,128)} async-done(((f32[128,128]{0,1:T(8,128)}), f32[128,128]{0,1:T(8,128)}) %all-reduce.2.cloned.1.call-update) | async-done | bytes 65552 | tf_op jit(solution)/shard_map/psum | solution.py:70
  791.1 1.6 copy.98
  792.7 0.4 multiply_bitcast_fusion
  793.1 0.1 fusion.20
  793.2 1.0 fusion.18
  794.2 33.7 %all-gather.2.cloned.1.call-done = bf16[1,64,128,128]{3,2,0,1:T(8,128)(2,1)} async-done(((bf16[1,1,128,128]{3,2,0,1:T(8,128)(2,1)}), bf16[1,64,128,128]{3,2,0,1:T(8,128)(2,1)}) %all-gather.2.cloned.1.call-update) | async-done | bytes 2097168 | tf_op jit(solution)/shard_map/all_gather | solution.py:124
  827.9 2.1 fusion.13
  830.0 0.9 fusion.3
  (24 shorter events, 0.4 us)
Async XLA Ops:
  8.0 358.4 %copy-start = (bf16[1,8,2,128,128]{4,3,2,1,0:T(8,128)(2,1)S(1)}, bf16[1,8,2,128,128]{4,3,2,1,0:T(8,128)(2,1)}, u32[]{:S(2)}) copy-start(bf16[1,8,2,128,128]{4,3,2,1,0:T(8,128)(2,1)} %param.8) | copy-start | bytes 1572868
  10.9 28.2 %all-to-all-start = ((bf16[2,1,64,8,128]{4,3,1,0,2:T(8,128)(2,1)}), bf16[2,1,64,8,128]{4,3,1,0,2:T(8,128)(2,1)S(1)}, u32[]{:S(2)}, u32[]{:S(2)}) async-start(bf16[2,1,64,8,128]{4,3,1,0,2:T(8,128)(2,1)} %pad_maximum_fusion), calls=%async_computation | async-start | bytes 524288 | tf_op jit(solution)/shard_map/all_to_all | solution.py:72
  40.0 12.2 %all-to-all-start.1 = ((bf16[2,1,1,128,128]{4,0,2,1,3:T(2,128)(2,1)}), bf16[2,1,1,128,128]{4,0,2,1,3:T(2,128)(2,1)S(1)}, u32[]{:S(2)}, u32[]{:S(2)}) async-start(bf16[2,1,1,128,128]{4,0,2,1,3:T(2,128)(2,1)} %copy.85), calls=%async_computation.1 | async-start | bytes 131072 | tf_op jit(solution)/shard_map/all_to_all | solution.py:73
  46.6 319.1 %reduce-scatter.2.cloned.1.call-start = ((), (), s32[]{:S(2)}) async-start(), calls=%async_computation.4 | async-start | bytes 1064960 | tf_op jit(solution)/shard_map/reduce_scatter | solution.py:85
  52.6 473.8 %copy-start.2 = (bf16[1,64,8,128]{3,2,1,0:T(8,128)(2,1)S(1)}, bf16[1,64,8,128]{3,2,1,0:T(8,128)(2,1)}, u32[]{:S(2)}) copy-start(bf16[1,64,8,128]{3,2,1,0:T(8,128)(2,1)} %param.5) | copy-start | bytes 393220
  520.1 11.8 %all-to-all-start.2 = ((bf16[1,8,16,128]{3,2,0,1:T(8,128)(2,1)}), bf16[1,8,16,128]{3,2,0,1:T(8,128)(2,1)S(1)}, u32[]{:S(2)}, u32[]{:S(2)}) async-start(bf16[1,8,16,128]{3,2,0,1:T(8,128)(2,1)} %copy.95), calls=%async_computation.3 | async-start | bytes 65536 | tf_op jit(solution)/shard_map/all_to_all | solution.py:120
  526.4 264.7 %all-reduce.2.cloned.1.call-start = ((), (), s32[]{:S(2)}) async-start(), calls=%async_computation.6 | async-start | bytes 131072 | tf_op jit(solution)/shard_map/psum | solution.py:70
  527.3 300.6 %all-gather.2.cloned.1.call-start = ((), (), s32[]{:S(2)}) async-start(), calls=%async_computation.5 | async-start | bytes 2129920 | tf_op jit(solution)/shard_map/all_gather | solution.py:124
  531.9 0.6 copy-start.1
  793.2 36.8 %copy-start.3 = (bf16[128,128]{1,0:T(8,128)(2,1)S(1)}, bf16[128,128]{1,0:T(8,128)(2,1)}, u32[]{:S(2)}) copy-start(bf16[128,128]{1,0:T(8,128)(2,1)} %param.9) | copy-start | bytes 98308
Sparse Core Ops, SparseCore 0:
  54.4 311.3 reduce-scatter.1
  532.6 295.2 all-gather.1
Sparse Core Ops, SparseCore 1:
  533.2 257.9 all-reduce.1
where the time goes:
time: 839 us; the launch traced here: 838 us
  waiting for transfers between devices  530 us (63%)
  blocking collectives  249 us (30%)
  starting transfers between devices  27.7 us (3%)
  between operations  15.6 us (2%)
    reduce_scatter x1, waiting for transfers between devices, on_device(): lax.psum_scatter(jnp.einsum('qjpx,fbxkpc->jfbkqc', table, split_pairs, pr...  311 us
    psum x1, waiting for transfers between devices, on_device(): local_sum, bias_sum = lax.psum((local_term, bias_term), ('dp', 'space'))  162 us
    all_gather x1, blocking collectives, on_device(): lax.all_gather(mode_back, 'dp', axis=1, tiled=True)  152 us
    psum x1, blocking collectives, on_device(): local_sum, bias_sum = lax.psum((local_term, bias_term), ('dp', 'space'))  96.2 us
    all_gather x1, waiting for transfers between devices, on_device(): slab_lines = lax.all_gather(lines_back, 'dp', axis=1, tiled=True)  33.7 us
  transfers between devices with their start and end apart: 6, of which 6 were waited for; matrix products, arithmetic and copies ran while one was open for 1% of the time, Pallas kernels for 0%

commit v1 on v0

v1 whole, which is shorter than its diff:
```python
import math

import jax
import jax.numpy as jnp
import numpy as np
from jax import lax
from jax.experimental import pallas as pl
from jax.experimental.pallas import tpu as pltpu
from jax.sharding import PartitionSpec as P

root_two_pi = 0.7978845608028654
cubic_coef = 0.044715

N = 8
C = 128
GRID = 512
MODES = 64
f32 = jnp.float32
bf16 = jnp.bfloat16

FIELDS, SPEC_Z, SPEC_YX, PARTIAL, BACK, BACK_YX, BACK_Z, ROWS, SUM_SPACE, SUM_Z, SUM_YX, SUM_BACK = range(12)


def gelu_slope(values):
    tangent = jnp.tanh(root_two_pi * (values + cubic_coef * values * values * values))
    return 0.5 * (1.0 + tangent) + 0.5 * values * (1.0 - tangent * tangent) * root_two_pi * (
        1.0 + 3.0 * cubic_coef * values * values
    )


def trig(phases):
    angles = (phases % GRID).astype(np.float32) * np.float32(2.0 * math.pi / GRID)
    return np.cos(angles), np.sin(angles)


def tables():
    j = (np.arange(N)[None, :] * N + np.arange(N)[:, None]).reshape(MODES)
    frequency = np.where(j < MODES // 2, j, j - MODES)
    c, s = trig(frequency[:, None] * np.arange(GRID)[None, :])
    x_table = np.stack([c, s], axis=1).reshape(2 * MODES, GRID)
    y = np.arange(MODES)[None, :] * N + np.arange(N)[:, None]
    c, s = trig(np.arange(MODES)[None, :, None] * y[:, None, :])
    y_table = np.stack([np.stack([c, -s], axis=3), np.stack([-s, -c], axis=3)], axis=2)
    y_table = y_table.reshape(N, 2 * MODES, 2 * MODES)
    y_tables = np.stack([y_table, np.swapaxes(y_table, 1, 2)], axis=1)
    order = np.arange(2 * MODES).reshape(N, N, 2).swapaxes(0, 1).reshape(-1)
    swap = np.eye(2 * MODES)[order]
    return [t.astype(bf16) for t in (x_table, np.ascontiguousarray(x_table.T), y_tables, swap)]


def dot(a, b):
    return jnp.dot(a, b, preferred_element_type=f32)


def dot_nt(a, b):
    return lax.dot_general(a, b, (((1,), (1,)), ((), ())), preferred_element_type=f32)


def kernel(
    field_hbm, pre_hbm, cot_hbm, weight_hbm, lw_hbm, xt_hbm, xtt_hbm, yt_hbm, swap_hbm,
    out_grad, out_spec, out_local, out_bias,
    field_v, pre_v, cot_v, weight, lw, xt, xtt, yt, swap,
    rows_f, rows_d, send1, recv1, local_part,
    send2, recv2, send3, recv3, send4, recv4, send5, recv5, send6, recv6, send7, recv7, send8, recv8,
    sum_send, sum_recv, sumz_send, sumz_recv, sumy_send, sumy_recv, sumb_send, sumb_recv,
    grads, in_sem, out_sem, send_sem, recv_sem,
):
    sp = lax.axis_index("space")
    dp = lax.axis_index("dp")
    yx = dp // N
    z = dp - yx * N

    def peer(axis, o):
        if axis == "space":
            other = lax.rem(sp + o, N)
            return other, sp, {"dp": dp, "space": other}
        if axis == "z":
            other = lax.rem(z + o, N)
            return other, z, {"dp": yx * N + other, "space": sp}
        other = lax.rem(yx + o, N)
        return other, yx, {"dp": other * N + z, "space": sp}

    barrier = pltpu.get_barrier_semaphore()
    for o in range(1, N):
        for axis in ("space", "z", "yx"):
            pl.semaphore_signal(barrier, inc=1, device_id=peer(axis, o)[2])

    loads = []
    for i, (src, dst) in enumerate((
        (pre_hbm.at[0], pre_v), (cot_hbm.at[0], cot_v), (field_hbm.at[0], field_v), (xt_hbm, xt),
        (lw_hbm, lw), (swap_hbm, swap), (yt_hbm.at[sp], yt), (weight_hbm, weight), (xtt_hbm, xtt),
    )):
        loads.append(pltpu.make_async_copy(src, dst, in_sem.at[i]))
        loads[-1].start()

    started = []

    def send(hop, axis, o, src, dst, each):
        other, me, device = peer(axis, o)
        copy = pltpu.make_async_remote_copy(
            src_ref=src.at[other] if each else src,
            dst_ref=dst.at[me],
            send_sem=send_sem.at[hop, o],
            recv_sem=recv_sem.at[hop, me],
            device_id=device,
        )
        copy.start()
        started.append(copy)

    def send_all(hop, axis, src, dst, each=True):
        for o in range(1, N):
            send(hop, axis, o, src, dst, each)
        me = peer(axis, 0)[1]
        dst[me] = src[me] if each else src[...]

    def wait_all(hop, axis, dst):
        for o in range(1, N):
            other, me, device = peer(axis, o)
            pltpu.make_async_remote_copy(
                src_ref=dst.at[other],
                dst_ref=dst.at[other],
                send_sem=send_sem.at[hop, o],
                recv_sem=recv_sem.at[hop, other],
                device_id=device,
            ).wait_recv()

    def total(ref):
        acc = ref[0]
        for i in range(1, N):
            acc = acc + ref[i]
        return acc

    for i in range(3):
        loads[i].wait()
    delta = (cot_v[...].astype(f32) * gelu_slope(pre_v[...].astype(f32))).astype(bf16).astype(f32)
    rows_d[...] = delta.reshape(GRID, C)
    rows_f[...] = field_v[...].astype(f32).reshape(GRID, C)
    bias_part = jnp.sum(delta, axis=0)
    for t in range(N):
        send1[t, :, 0:C] = rows_f[pl.ds(t, MODES, stride=N), :].astype(bf16)
        send1[t, :, C:] = rows_d[pl.ds(t, MODES, stride=N), :].astype(bf16)
    pl.semaphore_wait(barrier, 3 * (N - 1))
    send_all(FIELDS, "space", send1, recv1)

    both = send1[...].reshape(GRID, 2 * C)
    local = lax.dot_general(
        both[:, 0:C], both[:, C:], (((0,), (0,)), ((), ())), preferred_element_type=f32
    )
    for t in range(N):
        sum_send[t, 0:16, :] = local[16 * t : 16 * t + 16, :]
        sum_send[t, 16:24, :] = bias_part
    send_all(SUM_SPACE, "space", sum_send, sum_recv)
    for i in range(3, 9):
        loads[i].wait()
    local_part[...] = dot_nt(both[:, C:], lw[...]).reshape(N, MODES, C)

    wait_all(FIELDS, "space", recv1)
    send2[...] = dot(xt[...], recv1[...].reshape(GRID, 2 * C)).astype(bf16).reshape(N, 16, 2 * C)
    send_all(SPEC_Z, "z", send2, recv2)

    wait_all(SUM_SPACE, "space", sum_recv)
    sumz_send[...] = total(sum_recv)
    send_all(SUM_Z, "z", sumz_send, sumz_recv, each=False)

    wait_all(SPEC_Z, "z", recv2)
    send3[...] = dot(swap[...], recv2[...].reshape(2 * MODES, 2 * C)).astype(bf16).reshape(N, 16, 2 * C)
    send_all(SPEC_YX, "yx", send3, recv3)

    wait_all(SUM_Z, "z", sumz_recv)
    sumy_send[...] = total(sumz_recv)
    send_all(SUM_YX, "yx", sumy_send, sumy_recv, each=False)

    wait_all(SPEC_YX, "yx", recv3)
    send4[...] = dot(yt[0], recv3[...].reshape(2 * MODES, 2 * C)).reshape(N, 16, 2 * C)
    send_all(PARTIAL, "space", send4, recv4)

    wait_all(SUM_YX, "yx", sumy_recv)
    sums = total(sumy_recv)
    sumb_send[...] = sums[0:16]
    send_all(SUM_BACK, "space", sumb_send, sumb_recv, each=False)
    out_bias[...] = jnp.sum(sums[16:24], axis=0, keepdims=True)

    wait_all(PARTIAL, "space", recv4)
    spectra = total(recv4).astype(bf16)
    u_rows = spectra[:, 0:C]
    d_wide = spectra[:, C:].astype(f32)
    row = lax.broadcasted_iota(jnp.int32, (16, C), 0)
    even = row % 2 == 0
    d_turned = jnp.where(even, pltpu.roll(d_wide, 15, 0), -pltpu.roll(d_wide, 1, 0))
    scale = jnp.where((row // 2 == 0) & (sp == 0), 1.0, 2.0).astype(f32) / (GRID * GRID)
    d_both = jnp.concatenate([d_wide, d_turned], axis=0).astype(bf16)
    back = jnp.zeros((16, C), f32)
    for k in range(N):
        product = dot_nt(d_both, weight[k])
        back = jnp.where(row // 2 == k, product[0:16, 0:C] + product[16:32, C:], back)
    send5[...] = (back * scale).astype(bf16)
    send_all(BACK, "space", send5, recv5, each=False)

    d_pair = jnp.concatenate([d_wide, d_turned], axis=1)
    row2 = lax.broadcasted_iota(jnp.int32, (16, 2 * C), 0)
    for k in range(N):
        chosen = jnp.where(row2 // 2 == k, d_pair, 0.0).astype(bf16)
        product = lax.dot_general(
            u_rows, chosen, (((0,), (0,)), ((), ())), preferred_element_type=f32
        )
        scale_k = (jnp.where(sp == 0, 1.0, 2.0) if k == 0 else 2.0) / (GRID * GRID)
        grads[k] = (product * scale_k).astype(bf16)
    store = []
    for part in range(2):
        copy = pltpu.make_async_copy(
            grads.at[:, :, pl.ds(part * C, C)], out_spec.at[0, :, part], out_sem.at[part]
        )
        copy.start()
        store.append(copy)

    wait_all(BACK, "space", recv5)
    send6[...] = dot(yt[1], recv5[...].reshape(2 * MODES, C)).astype(bf16).reshape(N, 16, C)
    send_all(BACK_YX, "yx", send6, recv6)
    wait_all(BACK_YX, "yx", recv6)
    send7[...] = dot(swap[...], recv6[...].reshape(2 * MODES, C)).astype(bf16).reshape(N, 16, C)
    send_all(BACK_Z, "z", send7, recv7)
    wait_all(BACK_Z, "z", recv7)

    send8[...] = dot(xtt[...], recv7[...].reshape(2 * MODES, C)).astype(bf16).reshape(N, MODES, C)
    send_all(ROWS, "space", send8, recv8)

    wait_all(SUM_BACK, "space", sumb_recv)
    out_local[...] = sumb_recv[...].reshape(C, C)

    wait_all(ROWS, "space", recv8)
    for t in range(N):
        rows_f[pl.ds(t, MODES, stride=N), :] = recv8[t].astype(f32) + local_part[t]
    out_grad[...] = rows_f[...].reshape(1, MODES, N, C).astype(bf16)

    for copy in store:
        copy.wait()
    for copy in started:
        copy.wait_send()


def on_device(field_in, pre_act, cotangent, spec_weight, local_weight):
    x_table, x_back, y_tables, swap = (jnp.asarray(t) for t in tables())
    wide = (N, 16, 2 * C)
    slim = (N, 16, C)
    anywhere = pl.BlockSpec(memory_space=pl.ANY)
    in_vmem = pl.BlockSpec(memory_space=pltpu.VMEM)
    grad_input, grad_spectral, grad_local, grad_bias = pl.pallas_call(
        kernel,
        out_shape=(
            jax.ShapeDtypeStruct((1, MODES, N, C), bf16),
            jax.ShapeDtypeStruct((1, N, 2, C, C), bf16),
            jax.ShapeDtypeStruct((C, C), f32),
            jax.ShapeDtypeStruct((1, C), f32),
        ),
        in_specs=[anywhere] * 9,
        out_specs=(in_vmem, anywhere, in_vmem, in_vmem),
        scratch_shapes=[
            pltpu.VMEM((MODES, N, C), bf16),
            pltpu.VMEM((MODES, N, C), bf16),
            pltpu.VMEM((MODES, N, C), bf16),
            pltpu.VMEM((N, 2 * C, C), bf16),
            pltpu.VMEM((C, C), bf16),
            pltpu.VMEM((2 * MODES, GRID), bf16),
            pltpu.VMEM((GRID, 2 * MODES), bf16),
            pltpu.VMEM((2, 2 * MODES, 2 * MODES), bf16),
            pltpu.VMEM((2 * MODES, 2 * MODES), bf16),
            pltpu.VMEM((GRID, C), f32),
            pltpu.VMEM((GRID, C), f32),
            pltpu.VMEM((N, MODES, 2 * C), bf16),
            pltpu.VMEM((N, MODES, 2 * C), bf16),
            pltpu.VMEM((N, MODES, C), f32),
            pltpu.VMEM(wide, bf16),
            pltpu.VMEM(wide, bf16),
            pltpu.VMEM(wide, bf16),
            pltpu.VMEM(wide, bf16),
            pltpu.VMEM(wide, f32),
            pltpu.VMEM(wide, f32),
            pltpu.VMEM((16, C), bf16),
            pltpu.VMEM(slim, bf16),
            pltpu.VMEM(slim, bf16),
            pltpu.VMEM(slim, bf16),
            pltpu.VMEM(slim, bf16),
            pltpu.VMEM(slim, bf16),
            pltpu.VMEM((N, MODES, C), bf16),
            pltpu.VMEM((N, MODES, C), bf16),
            pltpu.VMEM((N, 24, C), f32),
            pltpu.VMEM((N, 24, C), f32),
            pltpu.VMEM((24, C), f32),
            pltpu.VMEM((N, 24, C), f32),
            pltpu.VMEM((24, C), f32),
            pltpu.VMEM((N, 24, C), f32),
            pltpu.VMEM((16, C), f32),
            pltpu.VMEM((N, 16, C), f32),
            pltpu.VMEM((N, C, 2 * C), bf16),
            pltpu.SemaphoreType.DMA((9,)),
            pltpu.SemaphoreType.DMA((2,)),
            pltpu.SemaphoreType.DMA((12, N)),
            pltpu.SemaphoreType.DMA((12, N)),
        ],
        compiler_params=pltpu.CompilerParams(
            collective_id=0, has_side_effects=True, vmem_limit_bytes=32 * 1024 * 1024
        ),
        cost_estimate=pl.CostEstimate(
            flops=250_000_000, bytes_accessed=2_500_000, transcendentals=65536
        ),
    )(
        field_in, pre_act, cotangent, spec_weight.reshape(N, 2 * C, C), local_weight,
        x_table, x_back, y_tables, swap,
    )
    return grad_input, grad_spectral, grad_local, grad_bias.reshape(C)


def solution(mesh):
    placed = (
        P(None, "space", "dp", None),
        P(None, "space", "dp", None),
        P(None, "space", "dp", None),
        P("dp", "space", None, None, None),
        P(),
    )
    return jax.shard_map(
        on_device,
        mesh=mesh,
        in_specs=placed,
        out_specs=(P(None, "space", "dp", None), P("dp", "space", None, None, None), P(), P()),
        check_vma=False,
    )
```

time: 839 us -> 72.5 us (0.09)
  the two profiles are of different devices: /device:TPU:16 before, /device:TPU:1 now
where the time goes in v1:
time: 72.5 us; the launch traced here: 72.1 us
  Pallas kernels  60.8 us (84%)
  local copies, waits for them, and re-layouts  10.7 us (15%)
    pallas_call x1, Pallas kernels, on_device(): pl.pallas_call(kernel, out_shape=(jax.ShapeDtypeStruct((1, MODES, N, C),...  60.8 us
    unnamed x22, local copies, waits for them, and re-layouts  10.7 us

profile of v1, /device:TPU:1, one launch (start us, length us, event | category | flops | bytes accessed | tf_op | source)
XLA Modules:
  0.0 72.1 jit_solution(15648592583751265348)
XLA Ops:
  0.6 0.0 copy-start
  0.6 1.0 %copy-done = bf16[1,8,2,128,128]{4,3,2,1,0:T(8,128)(2,1)S(1)} copy-done((bf16[1,8,2,128,128]{4,3,2,1,0:T(8,128)(2,1)S(1)}, bf16[1,8,2,128,128]{4,3,2,1,0:T(8,128)(2,1)}, u32[]{:S(2)}) %copy-start) | copy-done | bytes 524312
  1.7 0.0 copy-start.1
  1.7 1.0 %copy-done.1 = bf16[8,2,128,128]{3,2,1,0:T(8,128)(2,1)S(1)} copy-done((bf16[8,2,128,128]{3,2,1,0:T(8,128)(2,1)S(1)}, bf16[8,2,128,128]{3,2,1,0:T(8,128)(2,1)}, u32[]{:S(2)}) %copy-start.1) | copy-done | bytes 524312
  2.7 0.0 copy-start.2
  2.7 0.9 %copy-done.2 = bf16[1,64,8,128]{3,2,1,0:T(8,128)(2,1)S(1)} copy-done((bf16[1,64,8,128]{3,2,1,0:T(8,128)(2,1)S(1)}, bf16[1,64,8,128]{3,2,1,0:T(8,128)(2,1)}, u32[]{:S(2)}) %copy-start.2) | copy-done | bytes 131096
  3.6 0.0 copy-start.3
  3.6 0.9 %copy-done.3 = bf16[1,64,8,128]{3,2,1,0:T(8,128)(2,1)S(1)} copy-done((bf16[1,64,8,128]{3,2,1,0:T(8,128)(2,1)S(1)}, bf16[1,64,8,128]{3,2,1,0:T(8,128)(2,1)}, u32[]{:S(2)}) %copy-start.3) | copy-done | bytes 131096
  4.5 0.0 copy-start.4
  4.5 0.9 %copy-done.4 = bf16[1,64,8,128]{3,2,1,0:T(8,128)(2,1)S(1)} copy-done((bf16[1,64,8,128]{3,2,1,0:T(8,128)(2,1)S(1)}, bf16[1,64,8,128]{3,2,1,0:T(8,128)(2,1)}, u32[]{:S(2)}) %copy-start.4) | copy-done | bytes 131096
  5.4 0.0 copy-start.5
  5.4 0.9 %copy-done.5 = bf16[512,128]{1,0:T(8,128)(2,1)S(1)} copy-done((bf16[512,128]{1,0:T(8,128)(2,1)S(1)}, bf16[512,128]{1,0:T(8,128)(2,1)}, u32[]{:S(2)}) %copy-start.5) | copy-done | bytes 131096
  6.3 0.0 copy-start.6
  6.3 0.9 %copy-done.6 = bf16[128,512]{1,0:T(8,128)(2,1)S(1)} copy-done((bf16[128,512]{1,0:T(8,128)(2,1)S(1)}, bf16[128,512]{1,0:T(8,128)(2,1)}, u32[]{:S(2)}) %copy-start.6) | copy-done | bytes 131096
  7.2 0.0 copy-start.7
  7.2 0.8 %copy-done.7 = bf16[128,128]{1,0:T(8,128)(2,1)S(1)} copy-done((bf16[128,128]{1,0:T(8,128)(2,1)S(1)}, bf16[128,128]{1,0:T(8,128)(2,1)}, u32[]{:S(2)}) %copy-start.7) | copy-done | bytes 32792
  8.0 0.0 copy-start.8
  8.0 0.8 %copy-done.8 = bf16[128,128]{1,0:T(8,128)(2,1)S(1)} copy-done((bf16[128,128]{1,0:T(8,128)(2,1)S(1)}, bf16[128,128]{1,0:T(8,128)(2,1)}, u32[]{:S(2)}) %copy-start.8) | copy-done | bytes 32792
  8.8 60.8 %shard_map.120 = (bf16[1,64,8,128]{3,2,1,0:T(8,128)(2,1)S(1)}, bf16[1,8,2,128,128]{4,3,2,1,0:T(8,128)(2,1)S(1)}, f32[128,128]{1,0:T(8,128)S(1)}, f32[1,128]{1,0:T(1,128)S(1)}) custom-call(bf16[1,64,8,128]{3,2,1,0:T(8,128)(2,1)S(1)} %copy-done.2, bf16[1,64,8,128]{3,2,1,0:T(8,128)(2,1)S(1)} %copy-done.3, bf16[1,64,8,128]{3,2,1,0:T(8,128)(2,1)S(1)} %copy-done.4, ...), custom_call_target="tpu_custom_call" | custom-call | flops 250000000 | bytes 2500000 | tf_op jit(solution)/shard_map/pallas_call | solution.py:247
  69.5 0.7 copy.17
  70.2 0.8 %copy.18 = bf16[1,8,2,128,128]{4,3,2,1,0:T(8,128)(2,1)} copy(bf16[1,8,2,128,128]{4,3,2,1,0:T(8,128)(2,1)S(1)} %get-tuple-element.17) | data formatting | bytes 1048576
  71.0 0.6 copy.19
  71.6 0.5 copy.20
Async XLA Ops:
  0.6 1.0 %copy-start = (bf16[1,8,2,128,128]{4,3,2,1,0:T(8,128)(2,1)S(1)}, bf16[1,8,2,128,128]{4,3,2,1,0:T(8,128)(2,1)}, u32[]{:S(2)}) copy-start(bf16[1,8,2,128,128]{4,3,2,1,0:T(8,128)(2,1)} %param.12) | copy-start | bytes 1572868
  1.7 1.0 %copy-start.1 = (bf16[8,2,128,128]{3,2,1,0:T(8,128)(2,1)S(1)}, bf16[8,2,128,128]{3,2,1,0:T(8,128)(2,1)}, u32[]{:S(2)}) copy-start(bf16[8,2,128,128]{3,2,1,0:T(8,128)(2,1)} %constant.10.clone.yt_hbm) | copy-start | bytes 1572868
  2.7 0.9 %copy-start.2 = (bf16[1,64,8,128]{3,2,1,0:T(8,128)(2,1)S(1)}, bf16[1,64,8,128]{3,2,1,0:T(8,128)(2,1)}, u32[]{:S(2)}) copy-start(bf16[1,64,8,128]{3,2,1,0:T(8,128)(2,1)} %field_hbm.1) | copy-start | bytes 393220
  3.6 0.9 %copy-start.3 = (bf16[1,64,8,128]{3,2,1,0:T(8,128)(2,1)S(1)}, bf16[1,64,8,128]{3,2,1,0:T(8,128)(2,1)}, u32[]{:S(2)}) copy-start(bf16[1,64,8,128]{3,2,1,0:T(8,128)(2,1)} %pre_hbm.1) | copy-start | bytes 393220
  4.5 0.9 %copy-start.4 = (bf16[1,64,8,128]{3,2,1,0:T(8,128)(2,1)S(1)}, bf16[1,64,8,128]{3,2,1,0:T(8,128)(2,1)}, u32[]{:S(2)}) copy-start(bf16[1,64,8,128]{3,2,1,0:T(8,128)(2,1)} %cot_hbm.1) | copy-start | bytes 393220
  5.4 0.9 %copy-start.5 = (bf16[512,128]{1,0:T(8,128)(2,1)S(1)}, bf16[512,128]{1,0:T(8,128)(2,1)}, u32[]{:S(2)}) copy-start(bf16[512,128]{1,0:T(8,128)(2,1)} %constant.9.clone.xtt_hbm) | copy-start | bytes 393220
  6.3 0.9 %copy-start.6 = (bf16[128,512]{1,0:T(8,128)(2,1)S(1)}, bf16[128,512]{1,0:T(8,128)(2,1)}, u32[]{:S(2)}) copy-start(bf16[128,512]{1,0:T(8,128)(2,1)} %constant.8.clone.xt_hbm) | copy-start | bytes 393220
  7.2 0.8 %copy-start.7 = (bf16[128,128]{1,0:T(8,128)(2,1)S(1)}, bf16[128,128]{1,0:T(8,128)(2,1)}, u32[]{:S(2)}) copy-start(bf16[128,128]{1,0:T(8,128)(2,1)} %lw_hbm.1) | copy-start | bytes 98308
  8.0 0.8 %copy-start.8 = (bf16[128,128]{1,0:T(8,128)(2,1)S(1)}, bf16[128,128]{1,0:T(8,128)(2,1)}, u32[]{:S(2)}) copy-start(bf16[128,128]{1,0:T(8,128)(2,1)} %constant.11.clone.swap_hbm) | copy-start | bytes 98308

commit v2 on v1

v2 whole, which is shorter than its diff:
```python
import math

import jax
import jax.numpy as jnp
import numpy as np
from jax import lax
from jax.experimental import pallas as pl
from jax.experimental.pallas import tpu as pltpu
from jax.sharding import PartitionSpec as P

root_two_pi = 0.7978845608028654
cubic_coef = 0.044715

N = 8
C = 128
GRID = 512
MODES = 64
COLS = 4
f32 = jnp.float32
bf16 = jnp.bfloat16

PARTIAL, BACK, SUM_SPACE, SUM_Z, SUM_YX, SUM_BACK = range(6)
FIELD, DELTA, ROWS, SPEC, GRAD = range(5)


def gelu_slope(values):
    tangent = jnp.tanh(root_two_pi * (values + cubic_coef * values * values * values))
    return 0.5 * (1.0 + tangent) + 0.5 * values * (1.0 - tangent * tangent) * root_two_pi * (
        1.0 + 3.0 * cubic_coef * values * values
    )


def trig(phases):
    angles = (phases % GRID).astype(np.float32) * np.float32(2.0 * math.pi / GRID)
    return np.cos(angles), np.sin(angles)


def tables():
    j = np.arange(MODES)
    frequency = np.where(j < MODES // 2, j, j - MODES)
    c, s = trig(frequency[:, None] * np.arange(GRID)[None, :])
    both = np.stack([c, s]).reshape(2, MODES, 4, 2 * MODES)
    x_table = both.transpose(2, 0, 1, 3).reshape(4, 2 * MODES, 2 * MODES)
    by_row = both.reshape(2, MODES, 4, 2, MODES).transpose(2, 3, 4, 1, 0)
    same = np.eye(COLS)
    x_back = np.einsum("hoxjp,tu->hotxjpu", by_row, same).reshape(4, GRID, GRID)
    y = np.arange(MODES)[None, :, None] * N + np.arange(2)[:, None, None] * COLS + np.arange(COLS)
    c, s = trig(np.arange(MODES)[None, :, None, None] * y[:, None])
    turn = np.stack([np.stack([c, -s], axis=-2), np.stack([-s, -c], axis=-2)], axis=2)
    y_table = np.einsum("okqdpt,fg->ofkqdgpt", turn, np.eye(2)).reshape(2, 4 * MODES, 2 * GRID)
    y_back = turn.transpose(0, 3, 4, 5, 1, 2).reshape(2, GRID, 2 * MODES)
    return [t.astype(bf16) for t in (x_table, y_table, y_back, x_back)]


def dot(a, b):
    return jnp.dot(a, b, preferred_element_type=f32)


def dot_nt(a, b):
    return lax.dot_general(a, b, (((1,), (1,)), ((), ())), preferred_element_type=f32)


def kernel(
    field_hbm, pre_hbm, cot_hbm, weight_hbm, lw_hbm, xt_hbm, yt_hbm, yb_hbm, xb_hbm,
    out_grad, out_spec, out_local, out_bias,
    field_v, pre_v, cot_v, weight, lw, xt, yt, yb, xb,
    rows_f, rows_d, local_part, swap_f, swap_d, held_f, held_d, stage,
    spec_send, spec_recv, part_send, part_recv, back_send, back_recv, grad_send, grad_recv,
    swap_rows, held_rows,
    sum_send, sum_recv, sumz_send, sumz_recv, sumy_send, sumy_recv, sumb_send, sumb_recv,
    grads, in_sem, out_sem, send_sem, recv_sem, wide_send, wide_recv,
):
    sp = lax.axis_index("space")
    dp = lax.axis_index("dp")
    yx = dp // N
    z = dp - yx * N
    row_chip = sp // 2
    core = sp - row_chip * 2
    twin = {"dp": dp, "space": row_chip * 2 + 1 - core}

    def peer(axis, o):
        if axis == "space":
            other = lax.rem(sp + o, N)
            return other, sp, {"dp": dp, "space": other}
        if axis == "z":
            other = lax.rem(z + o, N)
            return other, z, {"dp": yx * N + other, "space": sp}
        other = lax.rem(yx + o, N)
        return other, yx, {"dp": other * N + z, "space": sp}

    loads = []
    for i, (src, dst) in enumerate((
        (field_hbm.at[0], field_v), (pre_hbm.at[0], pre_v), (cot_hbm.at[0], cot_v),
        (xt_hbm.at[row_chip], xt), (lw_hbm, lw), (yt_hbm.at[core], yt),
        (weight_hbm, weight), (yb_hbm.at[core], yb), (xb_hbm.at[row_chip], xb),
    )):
        loads.append(pltpu.make_async_copy(src, dst, in_sem.at[i]))
        loads[-1].start()

    barrier = pltpu.get_barrier_semaphore()
    for o in range(1, N):
        pl.semaphore_signal(barrier, inc=1, device_id=peer("space", o)[2])

    def greet(o, carry):
        pl.semaphore_signal(
            barrier, inc=1, device_id={"dp": lax.rem(dp + o, MODES), "space": sp}
        )
        return carry

    lax.fori_loop(1, MODES, greet, 0)

    started = []

    def send_all(hop, axis, src, dst, each=True):
        for o in range(1, N):
            other, me, device = peer(axis, o)
            copy = pltpu.make_async_remote_copy(
                src_ref=src.at[other] if each else src,
                dst_ref=dst.at[me],
                send_sem=send_sem.at[hop, o],
                recv_sem=recv_sem.at[hop, me],
                device_id=device,
            )
            copy.start()
            started.append(copy)
        me = peer(axis, 0)[1]
        dst[me] = src[me] if each else src[...]

    def wait_all(hop, axis, dst):
        for o in range(1, N):
            other, me, device = peer(axis, o)
            pltpu.make_async_remote_copy(
                src_ref=dst.at[other],
                dst_ref=dst.at[other],
                send_sem=send_sem.at[hop, o],
                recv_sem=recv_sem.at[hop, other],
                device_id=device,
            ).wait_recv()

    def to_twin(hop, src, dst):
        copy = pltpu.make_async_remote_copy(
            src_ref=src, dst_ref=dst, send_sem=wide_send.at[hop], recv_sem=wide_recv.at[hop],
            device_id=twin,
        )
        copy.start()
        started.append(copy)
        return copy

    def to_all_dp(hop, src, dst):
        def step(o, carry):
            other = lax.rem(dp + o, MODES)
            pltpu.make_async_remote_copy(
                src_ref=src.at[other],
                dst_ref=dst.at[dp],
                send_sem=wide_send.at[hop],
                recv_sem=wide_recv.at[hop],
                device_id={"dp": other, "space": sp},
            ).start()
            return carry

        lax.fori_loop(1, MODES, step, 0)
        dst[dp] = src[dp]
        whole = pltpu.make_async_remote_copy(
            src_ref=src.at[pl.ds(0, MODES - 1)],
            dst_ref=dst.at[pl.ds(0, MODES - 1)],
            send_sem=wide_send.at[hop],
            recv_sem=wide_recv.at[hop],
            device_id={"dp": lax.rem(dp + 1, MODES), "space": sp},
        )
        started.append(whole)
        return whole

    def total(ref):
        acc = ref[0]
        for i in range(1, N):
            acc = acc + ref[i]
        return acc

    def split(rows, swap, held):
        for t in range(COLS):
            theirs = rows[pl.ds((1 - core) * COLS + t, MODES, stride=N), :]
            swap[:, t * C : (t + 1) * C] = theirs.astype(bf16)
        for t in range(COLS):
            mine = rows[pl.ds(core * COLS + t, MODES, stride=N), :]
            held[core, :, t * C : (t + 1) * C] = mine.astype(bf16)

    loads[0].wait()
    rows_f[...] = field_v[...].astype(f32).reshape(GRID, C)
    split(rows_f, swap_f, held_f)
    loads[1].wait()
    loads[2].wait()
    delta = (cot_v[...].astype(f32) * gelu_slope(pre_v[...].astype(f32))).astype(bf16)
    delta_wide = delta.astype(f32)
    rows_d[...] = delta_wide.reshape(GRID, C)
    split(rows_d, swap_d, held_d)
    pl.semaphore_wait(barrier, MODES - 1 + N - 1)
    field_copy = to_twin(FIELD, swap_f, held_f.at[core])
    delta_copy = to_twin(DELTA, swap_d, held_d.at[core])

    loads[3].wait()

    def transform(held, f):
        product = dot(xt[...], held[...].reshape(2 * MODES, COLS * C))
        for part in range(2):
            for t in range(COLS):
                stage[pl.ds(f * N + part * COLS + t, MODES, stride=2 * N), :] = product[
                    part * MODES : (part + 1) * MODES, t * C : (t + 1) * C
                ]

    field_copy.wait_recv()
    transform(held_f, 0)
    delta_copy.wait_recv()
    transform(held_d, 1)
    spec_send[...] = stage[...].astype(bf16).reshape(MODES, 2 * N, C)
    spec_copy = to_all_dp(SPEC, spec_send, spec_recv)

    field_rows = rows_f[...].astype(bf16)
    delta_rows = rows_d[...].astype(bf16)
    local = lax.dot_general(
        field_rows, delta_rows, (((0,), (0,)), ((), ())), preferred_element_type=f32
    )
    bias_part = jnp.sum(delta_wide, axis=0)
    for t in range(N):
        sum_send[t, 0:16, :] = local[16 * t : 16 * t + 16, :]
        sum_send[t, 16:24, :] = bias_part
    send_all(SUM_SPACE, "space", sum_send, sum_recv)
    for i in range(4, 9):
        loads[i].wait()
    local_part[...] = dot_nt(delta_rows, lw[...])

    spec_copy.wait_recv()
    product = dot(yt[...], spec_recv[...].reshape(2 * GRID, C))
    for f in range(2):
        part_send[:, f] = product[f * 2 * MODES : (f + 1) * 2 * MODES].reshape(N, 16, C)
    send_all(PARTIAL, "space", part_send, part_recv)

    wait_all(SUM_SPACE, "space", sum_recv)
    sumz_send[...] = total(sum_recv)
    send_all(SUM_Z, "z", sumz_send, sumz_recv, each=False)

    wait_all(PARTIAL, "space", part_recv)
    spectra = total(part_recv).astype(bf16)
    u_rows = spectra[0]
    d_wide = spectra[1].astype(f32)
    row = lax.broadcasted_iota(jnp.int32, (16, C), 0)
    even = row % 2 == 0
    d_turned = jnp.where(even, pltpu.roll(d_wide, 15, 0), -pltpu.roll(d_wide, 1, 0))
    scale = jnp.where((row // 2 == 0) & (sp == 0), 1.0, 2.0).astype(f32) / (GRID * GRID)
    d_both = jnp.concatenate([d_wide, d_turned], axis=0).astype(bf16)
    back = jnp.zeros((16, C), f32)
    for k in range(N):
        product = dot_nt(d_both, weight[k])
        back = jnp.where(row // 2 == k, product[0:16, 0:C] + product[16:32, C:], back)
    back_send[...] = (back * scale).astype(bf16)
    send_all(BACK, "space", back_send, back_recv, each=False)

    wait_all(SUM_Z, "z", sumz_recv)
    sumy_send[...] = total(sumz_recv)
    send_all(SUM_YX, "yx", sumy_send, sumy_recv, each=False)

    wait_all(BACK, "space", back_recv)
    grad_send[...] = dot(yb[...], back_recv[...].reshape(2 * MODES, C)).astype(bf16).reshape(MODES, N, C)
    grad_copy = to_all_dp(GRAD, grad_send, grad_recv)

    wait_all(SUM_YX, "yx", sumy_recv)
    sums = total(sumy_recv)
    sumb_send[...] = sums[0:16]
    send_all(SUM_BACK, "space", sumb_send, sumb_recv, each=False)
    out_bias[...] = jnp.sum(sums[16:24], axis=0, keepdims=True)

    d_pair = jnp.concatenate([d_wide, d_turned], axis=1)
    row2 = lax.broadcasted_iota(jnp.int32, (16, 2 * C), 0)
    for k in range(N):
        chosen = jnp.where(row2 // 2 == k, d_pair, 0.0).astype(bf16)
        product = lax.dot_general(
            u_rows, chosen, (((0,), (0,)), ((), ())), preferred_element_type=f32
        )
        scale_k = (jnp.where(sp == 0, 1.0, 2.0) if k == 0 else 2.0) / (GRID * GRID)
        for part in range(2):
            grads[k, part] = (product[:, part * C : (part + 1) * C] * scale_k).astype(bf16)
    store = pltpu.make_async_copy(grads, out_spec.at[0], out_sem.at[0])
    store.start()

    grad_copy.wait_recv()
    arrived = grad_recv[...].reshape(GRID, C)
    theirs = dot(xb[pl.ds((1 - core) * COLS * MODES, COLS * MODES), :], arrived)
    swap_rows[...] = theirs.astype(bf16).reshape(COLS, MODES, C)
    rows_copy = to_twin(ROWS, swap_rows, held_rows)
    mine = dot(xb[pl.ds(core * COLS * MODES, COLS * MODES), :], arrived)
    mine = mine.astype(bf16).astype(f32)
    for t in range(COLS):
        rows_f[pl.ds(core * COLS + t, MODES, stride=N), :] = mine[t * MODES : (t + 1) * MODES]

    wait_all(SUM_BACK, "space", sumb_recv)
    out_local[...] = sumb_recv[...].reshape(C, C)

    rows_copy.wait_recv()
    for t in range(COLS):
        rows_f[pl.ds((1 - core) * COLS + t, MODES, stride=N), :] = held_rows[t].astype(f32)
    out_grad[...] = (rows_f[...] + local_part[...]).reshape(1, MODES, N, C).astype(bf16)

    store.wait()
    for copy in started:
        copy.wait_send()


def finish(*refs):
    for i in range(4):
        refs[4 + i][...] = refs[i][...]


def on_device(field_in, pre_act, cotangent, spec_weight, local_weight):
    anywhere = pl.BlockSpec(memory_space=pl.ANY)
    in_vmem = pl.BlockSpec(memory_space=pltpu.VMEM)
    block = pltpu.VMEM((MODES, N, C), bf16)
    rows = pltpu.VMEM((GRID, C), f32)
    results = pl.pallas_call(
        kernel,
        out_shape=(
            jax.ShapeDtypeStruct((1, MODES, N, C), bf16),
            jax.ShapeDtypeStruct((1, N, 2, C, C), bf16),
            jax.ShapeDtypeStruct((C, C), f32),
            jax.ShapeDtypeStruct((1, C), f32),
        ),
        in_specs=[anywhere] * 9,
        out_specs=(in_vmem, anywhere, in_vmem, in_vmem),
        scratch_shapes=[
            block, block, block,
            pltpu.VMEM((N, 2 * C, C), bf16),
            pltpu.VMEM((C, C), bf16),
            pltpu.VMEM((2 * MODES, 2 * MODES), bf16),
            pltpu.VMEM((4 * MODES, 2 * GRID), bf16),
            pltpu.VMEM((GRID, 2 * MODES), bf16),
            pltpu.VMEM((GRID, GRID), bf16),
            rows, rows, rows,
            pltpu.VMEM((MODES, COLS * C), bf16),
            pltpu.VMEM((MODES, COLS * C), bf16),
            pltpu.VMEM((2, MODES, COLS * C), bf16),
            pltpu.VMEM((2, MODES, COLS * C), bf16),
            pltpu.VMEM((2 * GRID, C), f32),
            pltpu.VMEM((MODES, 2 * N, C), bf16),
            pltpu.VMEM((MODES, 2 * N, C), bf16),
            pltpu.VMEM((N, 2, 16, C), f32),
            pltpu.VMEM((N, 2, 16, C), f32),
            pltpu.VMEM((16, C), bf16),
            pltpu.VMEM((N, 16, C), bf16),
            block, block,
            pltpu.VMEM((COLS, MODES, C), bf16),
            pltpu.VMEM((COLS, MODES, C), bf16),
            pltpu.VMEM((N, 24, C), f32),
            pltpu.VMEM((N, 24, C), f32),
            pltpu.VMEM((24, C), f32),
            pltpu.VMEM((N, 24, C), f32),
            pltpu.VMEM((24, C), f32),
            pltpu.VMEM((N, 24, C), f32),
            pltpu.VMEM((16, C), f32),
            pltpu.VMEM((N, 16, C), f32),
            pltpu.VMEM((N, 2, C, C), bf16),
            pltpu.SemaphoreType.DMA((9,)),
            pltpu.SemaphoreType.DMA((1,)),
            pltpu.SemaphoreType.DMA((6, N)),
            pltpu.SemaphoreType.DMA((6, N)),
            pltpu.SemaphoreType.DMA((5,)),
            pltpu.SemaphoreType.DMA((5,)),
        ],
        compiler_params=pltpu.CompilerParams(
            collective_id=0, has_side_effects=True, vmem_limit_bytes=62 * 1024 * 1024
        ),
        cost_estimate=pl.CostEstimate(
            flops=250_000_000, bytes_accessed=2_500_000, transcendentals=65536
        ),
    )(
        field_in, pre_act, cotangent, spec_weight.reshape(N, 2 * C, C), local_weight,
        *(jnp.asarray(t) for t in tables()),
    )
    grad_input, grad_spectral, grad_local, grad_bias = pl.pallas_call(
        finish,
        out_shape=tuple(jax.ShapeDtypeStruct(r.shape, r.dtype) for r in results),
        in_specs=[in_vmem] * 4,
        out_specs=(in_vmem,) * 4,
        compiler_params=pltpu.CompilerParams(vmem_limit_bytes=62 * 1024 * 1024),
    )(*results)
    return grad_input, grad_spectral, grad_local, grad_bias.reshape(C)


def solution(mesh):
    placed = (
        P(None, "space", "dp", None),
        P(None, "space", "dp", None),
        P(None, "space", "dp", None),
        P("dp", "space", None, None, None),
        P(),
    )
    return jax.shard_map(
        on_device,
        mesh=mesh,
        in_specs=placed,
        out_specs=(P(None, "space", "dp", None), P("dp", "space", None, None, None), P(), P()),
        check_vma=False,
    )
```

time: 72.5 us -> 51.7 us (0.71)
  local copies, waits for them, and re-layouts: 10.7 us -> 0 us
  Pallas kernels: 60.8 us -> 50.9 us
    pallas_call x1, Pallas kernels: 60.8 us -> 48.9 us  [on_device(): pl.pallas_call(kernel, out_shape=(jax.ShapeDtypeStruct((1, MODES, N, C),...]
    unnamed x22 -> x0, local copies, waits for them, and re-layouts: 10.7 us -> none
    pallas_call x0 -> x1, Pallas kernels: none -> 1.95 us  [on_device(): pl.pallas_call(finish, out_shape=tuple((jax.ShapeDtypeStruct(r.shape, r.d...]
where the time goes in v2:
time: 51.7 us; the launch traced here: 51.5 us
  Pallas kernels  50.9 us (98%)
  between operations  0.64 us (1%)
    pallas_call x1, Pallas kernels, on_device(): pl.pallas_call(kernel, out_shape=(jax.ShapeDtypeStruct((1, MODES, N, C),...  48.9 us
    pallas_call x1, Pallas kernels, on_device(): pl.pallas_call(finish, out_shape=tuple((jax.ShapeDtypeStruct(r.shape, r.d...  1.95 us

profile of v2, /device:TPU:1, one launch (start us, length us, event | category | flops | bytes accessed | tf_op | source)
XLA Modules:
  0.0 51.5 jit_solution(14336905202432105355)
XLA Ops:
  0.6 48.9 %shard_map.120 = (bf16[1,64,8,128]{3,2,1,0:T(8,128)(2,1)}, bf16[1,8,2,128,128]{4,3,2,1,0:T(8,128)(2,1)}, f32[128,128]{1,0:T(8,128)}, f32[1,128]{1,0:T(1,128)}) custom-call(bf16[1,64,8,128]{3,2,1,0:T(8,128)(2,1)} %field_hbm.1, bf16[1,64,8,128]{3,2,1,0:T(8,128)(2,1)} %pre_hbm.1, bf16[1,64,8,128]{3,2,1,0:T(8,128)(2,1)} %cot_hbm.1, ...), custom_call_target="tpu_custom_call" | custom-call | flops 250000000 | bytes 2500000 | tf_op jit(solution)/shard_map/pallas_call | solution.py:317
  49.6 2.0 %shard_map.121 = (bf16[1,64,8,128]{3,2,1,0:T(8,128)(2,1)}, bf16[1,8,2,128,128]{4,3,2,1,0:T(8,128)(2,1)}, f32[128,128]{1,0:T(8,128)}, f32[1,128]{1,0:T(1,128)}) custom-call(bf16[1,64,8,128]{3,2,1,0:T(8,128)(2,1)} %get-tuple-element.12.refs_0_, bf16[1,8,2,128,128]{4,3,2,1,0:T(8,128)(2,1)} %get-tuple-element.13.refs_1_, f32[128,128]{1,0:T(8,128)} %get-tuple-element.14.refs_2_, ...), custom_call_target="tpu_custom_call" | custom-call | tf_op jit(solution)/shard_map/pallas_call | solution.py:376

commit v3 on v2

--- a/solution.py
+++ b/solution.py
@@ -19,6 +19,13 @@
 f32 = jnp.float32
 bf16 = jnp.bfloat16
 
+Z_ORDER = [4, 3, 5, 2, 6, 1, 7]
+YX_ORDER = [(1, 2), (0, 2), (1, 1), (1, 3), (0, 1), (0, 3), (1, 0)]
+SPACE_ORDER = [(2, 0), (2, 1), (1, 0), (3, 0), (1, 1), (3, 1), (0, 1)]
+DP_ORDER = sorted(
+    [(l, x, z) for l in range(2) for x in range(4) for z in range(8) if l or x or z],
+    key=lambda o: -(o[0] + min(o[1], 4 - o[1]) + min(o[2], 8 - o[2])),
+)
 PARTIAL, BACK, SUM_SPACE, SUM_Z, SUM_YX, SUM_BACK = range(6)
 FIELD, DELTA, ROWS, SPEC, GRAD = range(5)
 
@@ -68,7 +75,7 @@
     spec_send, spec_recv, part_send, part_recv, back_send, back_recv, grad_send, grad_recv,
     swap_rows, held_rows,
     sum_send, sum_recv, sumz_send, sumz_recv, sumy_send, sumy_recv, sumb_send, sumb_recv,
-    grads, in_sem, out_sem, send_sem, recv_sem, wide_send, wide_recv,
+    in_sem, send_sem, recv_sem, wide_send, wide_recv, lines_in,
 ):
     sp = lax.axis_index("space")
     dp = lax.axis_index("dp")
@@ -80,13 +87,20 @@
 
     def peer(axis, o):
         if axis == "space":
-            other = lax.rem(sp + o, N)
+            chip, side = SPACE_ORDER[o - 1]
+            other = lax.rem(row_chip + chip, 4) * 2 + lax.rem(core + side, 2)
             return other, sp, {"dp": dp, "space": other}
         if axis == "z":
-            other = lax.rem(z + o, N)
+            other = lax.rem(z + Z_ORDER[o - 1], N)
             return other, z, {"dp": yx * N + other, "space": sp}
-        other = lax.rem(yx + o, N)
+        low, x = YX_ORDER[o - 1]
+        other = lax.rem(yx // 4 + low, 2) * 4 + lax.rem(yx % 4 + x, 4)
         return other, yx, {"dp": other * N + z, "space": sp}
+
+    def dp_peer(offset):
+        low, x, deep = offset
+        chips = lax.rem(yx // 4 + low, 2) * 4 + lax.rem(yx % 4 + x, 4)
+        return chips * N + lax.rem(z + deep, N)
 
     loads = []
     for i, (src, dst) in enumerate((
@@ -101,13 +115,9 @@
     for o in range(1, N):
         pl.semaphore_signal(barrier, inc=1, device_id=peer("space", o)[2])
 
-    def greet(o, carry):
-        pl.semaphore_signal(
-            barrier, inc=1, device_id={"dp": lax.rem(dp + o, MODES), "space": sp}
-        )
-        return carry
-
-    lax.fori_loop(1, MODES, greet, 0)
+    for o in range(1, N):
+        for axis in ("z", "yx"):
+            pl.semaphore_signal(barrier, inc=1, device_id=peer(axis, o)[2])
 
     started = []
 
@@ -123,7 +133,7 @@
             )
             copy.start()
             started.append(copy)
-        me = peer(axis, 0)[1]
+        me = {"space": sp, "z": z, "yx": yx}[axis]
         dst[me] = src[me] if each else src[...]
 
     def wait_all(hop, axis, dst):
@@ -147,8 +157,8 @@
         return copy
 
     def to_all_dp(hop, src, dst):
-        def step(o, carry):
-            other = lax.rem(dp + o, MODES)
+        for offset in DP_ORDER:
+            other = dp_peer(offset)
             pltpu.make_async_remote_copy(
                 src_ref=src.at[other],
                 dst_ref=dst.at[dp],
@@ -156,9 +166,6 @@
                 recv_sem=wide_recv.at[hop],
                 device_id={"dp": other, "space": sp},
             ).start()
-            return carry
-
-        lax.fori_loop(1, MODES, step, 0)
         dst[dp] = src[dp]
         whole = pltpu.make_async_remote_copy(
             src_ref=src.at[pl.ds(0, MODES - 1)],
@@ -193,7 +200,9 @@
     delta_wide = delta.astype(f32)
     rows_d[...] = delta_wide.reshape(GRID, C)
     split(rows_d, swap_d, held_d)
-    pl.semaphore_wait(barrier, MODES - 1 + N - 1)
+    pl.semaphore_wait(barrier, 3 * (N - 1))
+    for o in range(1, N):
+        pl.semaphore_signal(lines_in, inc=1, device_id=peer("yx", o)[2])
     field_copy = to_twin(FIELD, swap_f, held_f.at[core])
     delta_copy = to_twin(DELTA, swap_d, held_d.at[core])
 
@@ -212,6 +221,7 @@
     delta_copy.wait_recv()
     transform(held_d, 1)
     spec_send[...] = stage[...].astype(bf16).reshape(MODES, 2 * N, C)
+    pl.semaphore_wait(lines_in, N - 1)
     spec_copy = to_all_dp(SPEC, spec_send, spec_recv)
 
     field_rows = rows_f[...].astype(bf16)
@@ -277,9 +287,8 @@
         )
         scale_k = (jnp.where(sp == 0, 1.0, 2.0) if k == 0 else 2.0) / (GRID * GRID)
         for part in range(2):
-            grads[k, part] = (product[:, part * C : (part + 1) * C] * scale_k).astype(bf16)
-    store = pltpu.make_async_copy(grads, out_spec.at[0], out_sem.at[0])
-    store.start()
+            out_spec[0, k, part] = (product[:, part * C : (part + 1) * C] * scale_k).astype(bf16)
+
 
     grad_copy.wait_recv()
     arrived = grad_recv[...].reshape(GRID, C)
@@ -299,14 +308,16 @@
         rows_f[pl.ds((1 - core) * COLS + t, MODES, stride=N), :] = held_rows[t].astype(f32)
     out_grad[...] = (rows_f[...] + local_part[...]).reshape(1, MODES, N, C).astype(bf16)
 
-    store.wait()
     for copy in started:
         copy.wait_send()
 
 
-def finish(*refs):
-    for i in range(4):
-        refs[4 + i][...] = refs[i][...]
+def hand_over(*refs):
+    copies = [pltpu.make_async_copy(refs[i], refs[4 + i], refs[-1].at[i]) for i in range(4)]
+    for copy in copies:
+        copy.start()
+    for copy in copies:
+        copy.wait()
 
 
 def on_device(field_in, pre_act, cotangent, spec_weight, local_weight):
@@ -317,13 +328,13 @@
     results = pl.pallas_call(
         kernel,
         out_shape=(
-            jax.ShapeDtypeStruct((1, MODES, N, C), bf16),
-            jax.ShapeDtypeStruct((1, N, 2, C, C), bf16),
-            jax.ShapeDtypeStruct((C, C), f32),
-            jax.ShapeDtypeStruct((1, C), f32),
+            pltpu.VMEM((1, MODES, N, C), bf16),
+            pltpu.VMEM((1, N, 2, C, C), bf16),
+            pltpu.VMEM((C, C), f32),
+            pltpu.VMEM((1, C), f32),
         ),
         in_specs=[anywhere] * 9,
-        out_specs=(in_vmem, anywhere, in_vmem, in_vmem),
+        out_specs=(in_vmem,) * 4,
         scratch_shapes=[
             block, block, block,
             pltpu.VMEM((N, 2 * C, C), bf16),
@@ -355,16 +366,15 @@
             pltpu.VMEM((N, 24, C), f32),
             pltpu.VMEM((16, C), f32),
             pltpu.VMEM((N, 16, C), f32),
-            pltpu.VMEM((N, 2, C, C), bf16),
             pltpu.SemaphoreType.DMA((9,)),
-            pltpu.SemaphoreType.DMA((1,)),
             pltpu.SemaphoreType.DMA((6, N)),
             pltpu.SemaphoreType.DMA((6, N)),
             pltpu.SemaphoreType.DMA((5,)),
             pltpu.SemaphoreType.DMA((5,)),
+            pltpu.SemaphoreType.REGULAR,
         ],
         compiler_params=pltpu.CompilerParams(
-            collective_id=0, has_side_effects=True, vmem_limit_bytes=62 * 1024 * 1024
+            collective_id=0, has_side_effects=True, vmem_limit_bytes=int(62 * 1024 * 1024)
         ),
         cost_estimate=pl.CostEstimate(
             flops=250_000_000, bytes_accessed=2_500_000, transcendentals=65536
@@ -374,11 +384,12 @@
         *(jnp.asarray(t) for t in tables()),
     )
     grad_input, grad_spectral, grad_local, grad_bias = pl.pallas_call(
-        finish,
+        hand_over,
         out_shape=tuple(jax.ShapeDtypeStruct(r.shape, r.dtype) for r in results),
         in_specs=[in_vmem] * 4,
-        out_specs=(in_vmem,) * 4,
-        compiler_params=pltpu.CompilerParams(vmem_limit_bytes=62 * 1024 * 1024),
+        out_specs=(anywhere,) * 4,
+        scratch_shapes=[pltpu.SemaphoreType.DMA((4,))],
+        compiler_params=pltpu.CompilerParams(vmem_limit_bytes=1024 * 1024),
     )(*results)
     return grad_input, grad_spectral, grad_local, grad_bias.reshape(C)
 

time: 51.7 us -> 47.7 us (0.923)
  Pallas kernels: 50.9 us -> 46.9 us
    pallas_call x2, Pallas kernels: 50.9 us -> 46.9 us  [the longest x1 46 us: on_device(): pl.pallas_call(kernel, out_shape=(pltpu.VMEM((1, MODES, N, C), bf16), plt...]
where the time goes in v3:
time: 47.7 us; the launch traced here: 47.5 us
  Pallas kernels  46.9 us (98%)
  between operations  0.64 us (1%)
    pallas_call x1, Pallas kernels, on_device(): pl.pallas_call(kernel, out_shape=(pltpu.VMEM((1, MODES, N, C), bf16), plt...  46 us

profile of v3, /device:TPU:1, one launch (start us, length us, event | category | flops | bytes accessed | tf_op | source)
XLA Modules:
  0.0 47.5 jit_solution(10730502220311765145)
XLA Ops:
  0.6 46.0 %shard_map.120 = (bf16[1,64,8,128]{3,2,1,0:T(8,128)(2,1)S(1)}, bf16[1,8,2,128,128]{4,3,2,1,0:T(8,128)(2,1)S(1)}, f32[128,128]{1,0:T(8,128)S(1)}, f32[1,128]{1,0:T(1,128)S(1)}) custom-call(bf16[1,64,8,128]{3,2,1,0:T(8,128)(2,1)} %field_hbm.1, bf16[1,64,8,128]{3,2,1,0:T(8,128)(2,1)} %pre_hbm.1, bf16[1,64,8,128]{3,2,1,0:T(8,128)(2,1)} %cot_hbm.1, ...), custom_call_target="tpu_custom_call" | custom-call | flops 250000000 | bytes 2500000 | tf_op jit(solution)/shard_map/pallas_call | solution.py:328
  46.7 0.9 %shard_map.121 = (bf16[1,64,8,128]{3,2,1,0:T(8,128)(2,1)}, bf16[1,8,2,128,128]{4,3,2,1,0:T(8,128)(2,1)}, f32[128,128]{1,0:T(8,128)}, f32[1,128]{1,0:T(1,128)}) custom-call(bf16[1,64,8,128]{3,2,1,0:T(8,128)(2,1)S(1)} %get-tuple-element.12.refs_0_, bf16[1,8,2,128,128]{4,3,2,1,0:T(8,128)(2,1)S(1)} %get-tuple-element.13.refs_1_, ...), custom_call_target="tpu_custom_call" | custom-call | tf_op jit(solution)/shard_map/pallas_call | solution.py:386

commit v4 on v3

--- a/solution.py
+++ b/solution.py
@@ -70,7 +70,7 @@
 def kernel(
     field_hbm, pre_hbm, cot_hbm, weight_hbm, lw_hbm, xt_hbm, yt_hbm, yb_hbm, xb_hbm,
     out_grad, out_spec, out_local, out_bias,
-    field_v, pre_v, cot_v, weight, lw, xt, yt, yb, xb,
+    field_v, pre_v, cot_v, weight, turned, lw, xt, yt, yb, xb,
     rows_f, rows_d, local_part, swap_f, swap_d, held_f, held_d, stage,
     spec_send, spec_recv, part_send, part_recv, back_send, back_recv, grad_send, grad_recv,
     swap_rows, held_rows,
@@ -109,15 +109,15 @@
         (weight_hbm, weight), (yb_hbm.at[core], yb), (xb_hbm.at[row_chip], xb),
     )):
         loads.append(pltpu.make_async_copy(src, dst, in_sem.at[i]))
-        loads[-1].start()
+    for load in loads[:3]:
+        load.start()
 
     barrier = pltpu.get_barrier_semaphore()
-    for o in range(1, N):
-        pl.semaphore_signal(barrier, inc=1, device_id=peer("space", o)[2])
-
-    for o in range(1, N):
-        for axis in ("z", "yx"):
+    for axis in ("z", "yx", "space"):
+        for o in range(1, N):
             pl.semaphore_signal(barrier, inc=1, device_id=peer(axis, o)[2])
+    for load in loads[3:]:
+        load.start()
 
     started = []
 
@@ -128,7 +128,7 @@
                 src_ref=src.at[other] if each else src,
                 dst_ref=dst.at[me],
                 send_sem=send_sem.at[hop, o],
-                recv_sem=recv_sem.at[hop, me],
+                recv_sem=recv_sem.at[hop],
                 device_id=device,
             )
             copy.start()
@@ -137,15 +137,14 @@
         dst[me] = src[me] if each else src[...]
 
     def wait_all(hop, axis, dst):
-        for o in range(1, N):
-            other, me, device = peer(axis, o)
-            pltpu.make_async_remote_copy(
-                src_ref=dst.at[other],
-                dst_ref=dst.at[other],
-                send_sem=send_sem.at[hop, o],
-                recv_sem=recv_sem.at[hop, other],
-                device_id=device,
-            ).wait_recv()
+        seven = dst.at[pl.ds(0, N - 1)]
+        pltpu.make_async_remote_copy(
+            src_ref=seven,
+            dst_ref=seven,
+            send_sem=send_sem.at[hop, 0],
+            recv_sem=recv_sem.at[hop],
+            device_id=twin,
+        ).wait_recv()
 
     def to_twin(hop, src, dst):
         copy = pltpu.make_async_remote_copy(
@@ -156,8 +155,12 @@
         started.append(copy)
         return copy
 
-    def to_all_dp(hop, src, dst):
-        for offset in DP_ORDER:
+    def to_all_dp(hop, src, dst, before_others=None):
+        on_lines = lambda o: o[2] == 0 or o[:2] == (0, 0)
+        order = DP_ORDER if before_others is None else sorted(DP_ORDER, key=lambda o: not on_lines(o))
+        for place, offset in enumerate(order):
+            if before_others is not None and place == 2 * (N - 1):
+                before_others()
             other = dp_peer(offset)
             pltpu.make_async_remote_copy(
                 src_ref=src.at[other],
@@ -201,10 +204,10 @@
     rows_d[...] = delta_wide.reshape(GRID, C)
     split(rows_d, swap_d, held_d)
     pl.semaphore_wait(barrier, 3 * (N - 1))
+    field_copy = to_twin(FIELD, swap_f, held_f.at[core])
+    delta_copy = to_twin(DELTA, swap_d, held_d.at[core])
     for o in range(1, N):
         pl.semaphore_signal(lines_in, inc=1, device_id=peer("yx", o)[2])
-    field_copy = to_twin(FIELD, swap_f, held_f.at[core])
-    delta_copy = to_twin(DELTA, swap_d, held_d.at[core])
 
     loads[3].wait()
 
@@ -221,8 +224,9 @@
     delta_copy.wait_recv()
     transform(held_d, 1)
     spec_send[...] = stage[...].astype(bf16).reshape(MODES, 2 * N, C)
-    pl.semaphore_wait(lines_in, N - 1)
-    spec_copy = to_all_dp(SPEC, spec_send, spec_recv)
+    spec_copy = to_all_dp(
+        SPEC, spec_send, spec_recv, lambda: pl.semaphore_wait(lines_in, N - 1)
+    )
 
     field_rows = rows_f[...].astype(bf16)
     delta_rows = rows_d[...].astype(bf16)
@@ -237,6 +241,8 @@
     for i in range(4, 9):
         loads[i].wait()
     local_part[...] = dot_nt(delta_rows, lw[...])
+    for k in range(N):
+        turned[k] = weight[k].T
 
     spec_copy.wait_recv()
     product = dot(yt[...], spec_recv[...].reshape(2 * GRID, C))
@@ -259,7 +265,7 @@
     d_both = jnp.concatenate([d_wide, d_turned], axis=0).astype(bf16)
     back = jnp.zeros((16, C), f32)
     for k in range(N):
-        product = dot_nt(d_both, weight[k])
+        product = dot(d_both, turned[k])
         back = jnp.where(row // 2 == k, product[0:16, 0:C] + product[16:32, C:], back)
     back_send[...] = (back * scale).astype(bf16)
     send_all(BACK, "space", back_send, back_recv, each=False)
@@ -338,6 +344,7 @@
         scratch_shapes=[
             block, block, block,
             pltpu.VMEM((N, 2 * C, C), bf16),
+            pltpu.VMEM((N, C, 2 * C), bf16),
             pltpu.VMEM((C, C), bf16),
             pltpu.VMEM((2 * MODES, 2 * MODES), bf16),
             pltpu.VMEM((4 * MODES, 2 * GRID), bf16),
@@ -368,7 +375,7 @@
             pltpu.VMEM((N, 16, C), f32),
             pltpu.SemaphoreType.DMA((9,)),
             pltpu.SemaphoreType.DMA((6, N)),
-            pltpu.SemaphoreType.DMA((6, N)),
+            pltpu.SemaphoreType.DMA((6,)),
             pltpu.SemaphoreType.DMA((5,)),
             pltpu.SemaphoreType.DMA((5,)),
             pltpu.SemaphoreType.REGULAR,

time: 47.7 us -> 47.2 us (0.990)
  Pallas kernels: 46.9 us -> 46.4 us
where the time goes in v4:
time: 47.2 us; the launch traced here: 47.1 us
  Pallas kernels  46.4 us (98%)
  between operations  0.64 us (1%)
    pallas_call x1, Pallas kernels, on_device(): pl.pallas_call(kernel, out_shape=(pltpu.VMEM((1, MODES, N, C), bf16), plt...  45.6 us

profile of v4, /device:TPU:1, one launch (start us, length us, event | category | flops | bytes accessed | tf_op | source)
XLA Modules:
  0.0 47.1 jit_solution(14231335120691902837)
XLA Ops:
  0.6 45.6 %shard_map.120 = (bf16[1,64,8,128]{3,2,1,0:T(8,128)(2,1)S(1)}, bf16[1,8,2,128,128]{4,3,2,1,0:T(8,128)(2,1)S(1)}, f32[128,128]{1,0:T(8,128)S(1)}, f32[1,128]{1,0:T(1,128)S(1)}) custom-call(bf16[1,64,8,128]{3,2,1,0:T(8,128)(2,1)} %field_hbm.1, bf16[1,64,8,128]{3,2,1,0:T(8,128)(2,1)} %pre_hbm.1, bf16[1,64,8,128]{3,2,1,0:T(8,128)(2,1)} %cot_hbm.1, ...), custom_call_target="tpu_custom_call" | custom-call | flops 250000000 | bytes 2500000 | tf_op jit(solution)/shard_map/pallas_call | solution.py:334
  46.2 0.9 %shard_map.121 = (bf16[1,64,8,128]{3,2,1,0:T(8,128)(2,1)}, bf16[1,8,2,128,128]{4,3,2,1,0:T(8,128)(2,1)}, f32[128,128]{1,0:T(8,128)}, f32[1,128]{1,0:T(1,128)}) custom-call(bf16[1,64,8,128]{3,2,1,0:T(8,128)(2,1)S(1)} %get-tuple-element.12.refs_0_, bf16[1,8,2,128,128]{4,3,2,1,0:T(8,128)(2,1)S(1)} %get-tuple-element.13.refs_1_, ...), custom_call_target="tpu_custom_call" | custom-call | tf_op jit(solution)/shard_map/pallas_call | solution.py:393

commit v5 on v4

--- a/solution.py
+++ b/solution.py
@@ -121,18 +121,30 @@
 
     started = []
 
+    def drain():
+        while started:
+            started.pop(0).wait_send()
+
+
     def send_all(hop, axis, src, dst, each=True):
         for o in range(1, N):
             other, me, device = peer(axis, o)
             copy = pltpu.make_async_remote_copy(
                 src_ref=src.at[other] if each else src,
                 dst_ref=dst.at[me],
-                send_sem=send_sem.at[hop, o],
+                send_sem=send_sem.at[hop],
                 recv_sem=recv_sem.at[hop],
                 device_id=device,
             )
             copy.start()
-            started.append(copy)
+        seven = dst.at[pl.ds(0, N - 1)]
+        started.append(pltpu.make_async_remote_copy(
+            src_ref=seven,
+            dst_ref=seven,
+            send_sem=send_sem.at[hop],
+            recv_sem=recv_sem.at[hop],
+            device_id=twin,
+        ))
         me = {"space": sp, "z": z, "yx": yx}[axis]
         dst[me] = src[me] if each else src[...]
 
@@ -141,7 +153,7 @@
         pltpu.make_async_remote_copy(
             src_ref=seven,
             dst_ref=seven,
-            send_sem=send_sem.at[hop, 0],
+            send_sem=send_sem.at[hop],
             recv_sem=recv_sem.at[hop],
             device_id=twin,
         ).wait_recv()
@@ -296,11 +308,13 @@
             out_spec[0, k, part] = (product[:, part * C : (part + 1) * C] * scale_k).astype(bf16)
 
 
+    drain()
     grad_copy.wait_recv()
     arrived = grad_recv[...].reshape(GRID, C)
     theirs = dot(xb[pl.ds((1 - core) * COLS * MODES, COLS * MODES), :], arrived)
     swap_rows[...] = theirs.astype(bf16).reshape(COLS, MODES, C)
     rows_copy = to_twin(ROWS, swap_rows, held_rows)
+    started.clear()
     mine = dot(xb[pl.ds(core * COLS * MODES, COLS * MODES), :], arrived)
     mine = mine.astype(bf16).astype(f32)
     for t in range(COLS):
@@ -309,13 +323,10 @@
     wait_all(SUM_BACK, "space", sumb_recv)
     out_local[...] = sumb_recv[...].reshape(C, C)
 
-    rows_copy.wait_recv()
+    rows_copy.wait()
     for t in range(COLS):
         rows_f[pl.ds((1 - core) * COLS + t, MODES, stride=N), :] = held_rows[t].astype(f32)
     out_grad[...] = (rows_f[...] + local_part[...]).reshape(1, MODES, N, C).astype(bf16)
-
-    for copy in started:
-        copy.wait_send()
 
 
 def hand_over(*refs):
@@ -374,7 +385,7 @@
             pltpu.VMEM((16, C), f32),
             pltpu.VMEM((N, 16, C), f32),
             pltpu.SemaphoreType.DMA((9,)),
-            pltpu.SemaphoreType.DMA((6, N)),
+            pltpu.SemaphoreType.DMA((6,)),
             pltpu.SemaphoreType.DMA((6,)),
             pltpu.SemaphoreType.DMA((5,)),
             pltpu.SemaphoreType.DMA((5,)),

time: 47.2 us -> 46.8 us (level)
  no operation moved by 1% of the time
where the time goes in v5:
time: 46.8 us; the launch traced here: 46.6 us
  Pallas kernels  46 us (98%)
  between operations  0.64 us (1%)
    pallas_call x1, Pallas kernels, on_device(): pl.pallas_call(kernel, out_shape=(pltpu.VMEM((1, MODES, N, C), bf16), plt...  45.1 us

profile of v5, /device:TPU:1, one launch (start us, length us, event | category | flops | bytes accessed | tf_op | source)
XLA Modules:
  0.0 46.6 jit_solution(1130076023099978433)
XLA Ops:
  0.6 45.1 %shard_map.120 = (bf16[1,64,8,128]{3,2,1,0:T(8,128)(2,1)S(1)}, bf16[1,8,2,128,128]{4,3,2,1,0:T(8,128)(2,1)S(1)}, f32[128,128]{1,0:T(8,128)S(1)}, f32[1,128]{1,0:T(1,128)S(1)}) custom-call(bf16[1,64,8,128]{3,2,1,0:T(8,128)(2,1)} %field_hbm.1, bf16[1,64,8,128]{3,2,1,0:T(8,128)(2,1)} %pre_hbm.1, bf16[1,64,8,128]{3,2,1,0:T(8,128)(2,1)} %cot_hbm.1, ...), custom_call_target="tpu_custom_call" | custom-call | flops 250000000 | bytes 2500000 | tf_op jit(solution)/shard_map/pallas_call | solution.py:345
  45.7 0.9 %shard_map.121 = (bf16[1,64,8,128]{3,2,1,0:T(8,128)(2,1)}, bf16[1,8,2,128,128]{4,3,2,1,0:T(8,128)(2,1)}, f32[128,128]{1,0:T(8,128)}, f32[1,128]{1,0:T(1,128)}) custom-call(bf16[1,64,8,128]{3,2,1,0:T(8,128)(2,1)S(1)} %get-tuple-element.12.refs_0_, bf16[1,8,2,128,128]{4,3,2,1,0:T(8,128)(2,1)S(1)} %get-tuple-element.13.refs_1_, ...), custom_call_target="tpu_custom_call" | custom-call | tf_op jit(solution)/shard_map/pallas_call | solution.py:404

commit v6 on v5

--- a/solution.py
+++ b/solution.py
@@ -54,7 +54,7 @@
     y = np.arange(MODES)[None, :, None] * N + np.arange(2)[:, None, None] * COLS + np.arange(COLS)
     c, s = trig(np.arange(MODES)[None, :, None, None] * y[:, None])
     turn = np.stack([np.stack([c, -s], axis=-2), np.stack([-s, -c], axis=-2)], axis=2)
-    y_table = np.einsum("okqdpt,fg->ofkqdgpt", turn, np.eye(2)).reshape(2, 4 * MODES, 2 * GRID)
+    y_table = turn.reshape(2, 2 * MODES, GRID)
     y_back = turn.transpose(0, 3, 4, 5, 1, 2).reshape(2, GRID, 2 * MODES)
     return [t.astype(bf16) for t in (x_table, y_table, y_back, x_back)]
 
@@ -198,36 +198,41 @@
             acc = acc + ref[i]
         return acc
 
-    def split(rows, swap, held):
+    def split(rows, swap):
         for t in range(COLS):
             theirs = rows[pl.ds((1 - core) * COLS + t, MODES, stride=N), :]
             swap[:, t * C : (t + 1) * C] = theirs.astype(bf16)
+
+    def keep(rows, held):
         for t in range(COLS):
             mine = rows[pl.ds(core * COLS + t, MODES, stride=N), :]
             held[core, :, t * C : (t + 1) * C] = mine.astype(bf16)
 
     loads[0].wait()
     rows_f[...] = field_v[...].astype(f32).reshape(GRID, C)
-    split(rows_f, swap_f, held_f)
+    split(rows_f, swap_f)
     loads[1].wait()
     loads[2].wait()
     delta = (cot_v[...].astype(f32) * gelu_slope(pre_v[...].astype(f32))).astype(bf16)
     delta_wide = delta.astype(f32)
     rows_d[...] = delta_wide.reshape(GRID, C)
-    split(rows_d, swap_d, held_d)
+    split(rows_d, swap_d)
     pl.semaphore_wait(barrier, 3 * (N - 1))
     field_copy = to_twin(FIELD, swap_f, held_f.at[core])
     delta_copy = to_twin(DELTA, swap_d, held_d.at[core])
     for o in range(1, N):
         pl.semaphore_signal(lines_in, inc=1, device_id=peer("yx", o)[2])
 
+    keep(rows_f, held_f)
+    keep(rows_d, held_d)
+
     loads[3].wait()
 
     def transform(held, f):
         product = dot(xt[...], held[...].reshape(2 * MODES, COLS * C))
         for part in range(2):
             for t in range(COLS):
-                stage[pl.ds(f * N + part * COLS + t, MODES, stride=2 * N), :] = product[
+                stage[f, pl.ds(part * COLS + t, MODES, stride=N), :] = product[
                     part * MODES : (part + 1) * MODES, t * C : (t + 1) * C
                 ]
 
@@ -235,7 +240,8 @@
     transform(held_f, 0)
     delta_copy.wait_recv()
     transform(held_d, 1)
-    spec_send[...] = stage[...].astype(bf16).reshape(MODES, 2 * N, C)
+    for f in range(2):
+        spec_send[:, :, f * C : (f + 1) * C] = stage[f].astype(bf16).reshape(MODES, N, C)
     spec_copy = to_all_dp(
         SPEC, spec_send, spec_recv, lambda: pl.semaphore_wait(lines_in, N - 1)
     )
@@ -257,9 +263,7 @@
         turned[k] = weight[k].T
 
     spec_copy.wait_recv()
-    product = dot(yt[...], spec_recv[...].reshape(2 * GRID, C))
-    for f in range(2):
-        part_send[:, f] = product[f * 2 * MODES : (f + 1) * 2 * MODES].reshape(N, 16, C)
+    part_send[...] = dot(yt[...], spec_recv[...].reshape(GRID, 2 * C)).reshape(N, 16, 2 * C)
     send_all(PARTIAL, "space", part_send, part_recv)
 
     wait_all(SUM_SPACE, "space", sum_recv)
@@ -268,8 +272,8 @@
 
     wait_all(PARTIAL, "space", part_recv)
     spectra = total(part_recv).astype(bf16)
-    u_rows = spectra[0]
-    d_wide = spectra[1].astype(f32)
+    u_rows = spectra[:, 0:C]
+    d_wide = spectra[:, C:].astype(f32)
     row = lax.broadcasted_iota(jnp.int32, (16, C), 0)
     even = row % 2 == 0
     d_turned = jnp.where(even, pltpu.roll(d_wide, 15, 0), -pltpu.roll(d_wide, 1, 0))
@@ -358,7 +362,7 @@
             pltpu.VMEM((N, C, 2 * C), bf16),
             pltpu.VMEM((C, C), bf16),
             pltpu.VMEM((2 * MODES, 2 * MODES), bf16),
-            pltpu.VMEM((4 * MODES, 2 * GRID), bf16),
+            pltpu.VMEM((2 * MODES, GRID), bf16),
             pltpu.VMEM((GRID, 2 * MODES), bf16),
             pltpu.VMEM((GRID, GRID), bf16),
             rows, rows, rows,
@@ -366,11 +370,11 @@
             pltpu.VMEM((MODES, COLS * C), bf16),
             pltpu.VMEM((2, MODES, COLS * C), bf16),
             pltpu.VMEM((2, MODES, COLS * C), bf16),
-            pltpu.VMEM((2 * GRID, C), f32),
-            pltpu.VMEM((MODES, 2 * N, C), bf16),
-            pltpu.VMEM((MODES, 2 * N, C), bf16),
-            pltpu.VMEM((N, 2, 16, C), f32),
-            pltpu.VMEM((N, 2, 16, C), f32),
+            pltpu.VMEM((2, GRID, C), f32),
+            pltpu.VMEM((MODES, N, 2 * C), bf16),
+            pltpu.VMEM((MODES, N, 2 * C), bf16),
+            pltpu.VMEM((N, 16, 2 * C), f32),
+            pltpu.VMEM((N, 16, 2 * C), f32),
             pltpu.VMEM((16, C), bf16),
             pltpu.VMEM((N, 16, C), bf16),
             block, block,

time: 46.8 us -> 46.7 us (level)
  no operation moved by 1% of the time
where the time goes in v6:
time: 46.7 us; the launch traced here: 46.6 us
  Pallas kernels  45.9 us (98%)
  between operations  0.64 us (1%)
    pallas_call x1, Pallas kernels, on_device(): pl.pallas_call(kernel, out_shape=(pltpu.VMEM((1, MODES, N, C), bf16), plt...  45 us

profile of v6, /device:TPU:1, one launch (start us, length us, event | category | flops | bytes accessed | tf_op | source)
XLA Modules:
  0.0 46.6 jit_solution(9254472221382371058)
XLA Ops:
  0.6 45.0 %shard_map.120 = (bf16[1,64,8,128]{3,2,1,0:T(8,128)(2,1)S(1)}, bf16[1,8,2,128,128]{4,3,2,1,0:T(8,128)(2,1)S(1)}, f32[128,128]{1,0:T(8,128)S(1)}, f32[1,128]{1,0:T(1,128)S(1)}) custom-call(bf16[1,64,8,128]{3,2,1,0:T(8,128)(2,1)} %field_hbm.1, bf16[1,64,8,128]{3,2,1,0:T(8,128)(2,1)} %pre_hbm.1, bf16[1,64,8,128]{3,2,1,0:T(8,128)(2,1)} %cot_hbm.1, ...), custom_call_target="tpu_custom_call" | custom-call | flops 250000000 | bytes 2500000 | tf_op jit(solution)/shard_map/pallas_call | solution.py:349
  45.7 0.9 %shard_map.121 = (bf16[1,64,8,128]{3,2,1,0:T(8,128)(2,1)}, bf16[1,8,2,128,128]{4,3,2,1,0:T(8,128)(2,1)}, f32[128,128]{1,0:T(8,128)}, f32[1,128]{1,0:T(1,128)}) custom-call(bf16[1,64,8,128]{3,2,1,0:T(8,128)(2,1)S(1)} %get-tuple-element.12.refs_0_, bf16[1,8,2,128,128]{4,3,2,1,0:T(8,128)(2,1)S(1)} %get-tuple-element.13.refs_1_, ...), custom_call_target="tpu_custom_call" | custom-call | tf_op jit(solution)/shard_map/pallas_call | solution.py:408
